TPU v7x, 512 devices: a whole 4x8x8 slice. The times are simulated.
512 devices in a mesh: section: 8 (over y), dp: 32 (over z_lo, x, core), tensor: 2 (over z_hi).
Axes of the slice: x: 4, y: 8, z: 8 (z_hi: 2, z_lo: 4; z = z_hi * 4 + z_lo), core: 2. Of those that a mesh axis runs over, the one named last changes fastest.
Arguments:
- context: bfloat16 [16384, 6144], P('dp', 'section'), may hold values from -64 to 64
- out_weight: bfloat16 [6144, 6144], P('section', ('tensor', 'dp')), may hold values from -0.078125 to 0.078125
- previous: bfloat16 [16384, 6144], P('dp', ('tensor', 'section')), may hold values from -64 to 64
- section_act: bfloat16 [8, 6144, 6144], P('section', 'dp', 'tensor'), may hold values from -6 to 6
- fresh_batch: bfloat16 [6144, 6144], P('dp', 'tensor'), may hold values from -6 to 6
- section_gains: float32 [8, 6144], P('section', 'tensor'), may hold values from 0.1 to 1.9
- mask_blocks: int32 [32, 12], P('dp'), may hold values from 0 to 15, all different within a row
Outputs:
- targets: bfloat16 [16384, 6144], P('dp', ('tensor', 'section'))
- section_out: bfloat16 [8, 6144, 6144], P('section', 'dp', 'tensor')
- target_error: float32 [6144, 6144], P('dp', ('tensor', 'section'))
Inputs may be any that keep to these rules, and one draw needn't show every extreme that they name: `mask_blocks`: each row names 12 different blocks.
All inputs are finite; a program needn't handle non-finite values.
Results may differ from a plain program's by a relative error of at most 0.015.
Values may be sent and summed in bfloat16 or wider, within the bound.
No kernel may reach another device: no remote copies, remote signals or barrier semaphores. Data moves between devices by JAX's collectives and lax.ppermute only.
A program may use at most 64 MiB of HBM per device.

v0:
```python
import jax
import jax.numpy as jnp
from jax import lax
from jax.sharding import PartitionSpec as P

GRID_SIDE = 16
BLOCK_SIDE = 4
PATCHES = 256


def shifted(value, axis, steps):
    count = lax.axis_size(axis)
    leading, last = (max(0, -steps), min(count, count - steps))
    return lax.ppermute(value, axis, [(source, source + steps) for source in range(leading, last)])


def spread_2(x, axis, root):
    mine = lax.axis_index(axis) == root
    return lax.psum(jnp.where(mine, x, jnp.zeros_like(x)), axis)


def instance_norm(values, images):
    shaped = values.reshape(images, -1, values.shape[-1])
    center = jnp.mean(shaped, axis=1, keepdims=True)
    spread = jnp.mean(jnp.square(shaped - center), axis=1, keepdims=True)
    return ((shaped - center) * lax.rsqrt(spread + 1e-05)).reshape(values.shape)


def masked_patches(mask_blocks):
    per_side = GRID_SIDE // BLOCK_SIDE
    within = jnp.arange(BLOCK_SIDE * BLOCK_SIDE, dtype=jnp.int32)
    chosen = mask_blocks[..., None]
    grid_row = chosen // per_side * BLOCK_SIDE + within // BLOCK_SIDE
    grid_col = chosen % per_side * BLOCK_SIDE + within % BLOCK_SIDE
    return grid_row * GRID_SIDE + grid_col


def on_device(context, out_weight, previous, section_act, fresh_batch, section_gains, mask_blocks):
    partial_sum = jnp.dot(
        context,
        lax.all_gather(out_weight, "dp", axis=1, tiled=True),
        preferred_element_type=jnp.float32,
    ).astype(jnp.bfloat16)
    width = previous.shape[1]
    position = lax.axis_index("section")
    sections = lax.axis_size("section")
    summed = lax.psum(partial_sum, "section").astype(jnp.float32)
    share = lax.dynamic_slice_in_dim(summed, position * width, width, 1)
    images = context.shape[0] // PATCHES
    normed_new = instance_norm(share, images)
    normed_old = instance_norm(previous.astype(jnp.float32), images)
    targets = (0.5 * (normed_new + normed_old)).astype(jnp.bfloat16)
    incoming = shifted(section_act, "section", 1)
    current = jnp.where(position == 0, fresh_batch[None], incoming).astype(jnp.float32)
    squares = lax.psum(jnp.sum(current * current, axis=-1), "tensor")
    features = current.shape[-1] * lax.axis_size("tensor")
    scaling = lax.rsqrt(squares[..., None] / features + 1e-06)
    section_out = (current * scaling * section_gains[:, None, :]).astype(jnp.bfloat16)
    predicted = spread_2(section_act[0], "section", sections - 1)
    own_columns = lax.dynamic_slice_in_dim(predicted, position * width, width, 1)
    patch_ids = masked_patches(mask_blocks[0]).reshape(-1)
    picked = jnp.take(targets, patch_ids, axis=0).astype(jnp.float32)
    target_error = own_columns.astype(jnp.float32) - picked
    return (targets, section_out, target_error)


def solution(mesh):
    in_specs = (
        P("dp", "section"),
        P("section", ("tensor", "dp")),
        P("dp", ("tensor", "section")),
        P("section", "dp", "tensor"),
        P("dp", "tensor"),
        P("section", "tensor"),
        P("dp", None),
    )
    out_specs = (
        P("dp", ("tensor", "section")),
        P("section", "dp", "tensor"),
        P("dp", ("tensor", "section")),
    )
    return jax.shard_map(
        on_device, mesh=mesh, in_specs=in_specs, out_specs=out_specs, check_vma=False
    )
```

profile of v0, /device:TPU:1, one launch (start us, length us, event | category | flops | bytes accessed | tf_op | source)
XLA Modules:
  0.0 233.4 jit_solution(17504914805390724261)
XLA Ops:
  7.2 0.0 copy-start
  7.2 0.0 all-gather.2.cloned.1.call-start
  7.2 0.7 all-gather.2.cloned.1.call-update
  7.9 0.0 all-reduce.3.cloned.1.call-start
  8.0 1.2 select_bitcast_fusion
  9.2 73.9 %all-gather.2.cloned.1.call-done = bf16[768,3072]{0,1:T(8,128)(2,1)} async-done(((bf16[768,96]{0,1:T(8,128)(2,1)}), bf16[768,3072]{0,1:T(8,128)(2,1)}) %all-gather.2.cloned.1.call-update) | async-done | bytes 4718608 | tf_op jit(solution)/shard_map/all_gather | solution.py:41
  83.1 0.0 copy-done
  83.1 6.3 %convolution_convert_fusion = bf16[512,3072]{1,0:T(8,128)(2,1)} fusion(bf16[512,768]{1,0:T(8,128)(2,1)S(1)} %copy-done, bf16[768,3072]{0,1:T(8,128)(2,1)} %all-gather.2.cloned.1.call-done), kind=kOutput, calls=%fused_computation.1 | convolution fusion | flops 2417491968 | bytes 8650752 | tf_op jit(solution)/shard_map/dot_general | solution.py:39
  89.4 0.0 all-reduce.3.cloned.1.call-update
  89.4 3.3 %collective-permute-start = (bf16[1,192,3072]{2,1,0:T(8,128)(2,1)}, bf16[1,192,3072]{2,1,0:T(8,128)(2,1)S(1)}, u32[]{:S(2)}, u32[]{:S(2)}) collective-permute-start(bf16[1,192,3072]{2,1,0:T(8,128)(2,1)} %param.10), channel_id=1, source_target_pairs={{0,64},{64,128},{128,192},{192,256},{256,320},{320,384},{384,448},... | collective-permute-start | bytes 3538952 | tf_op jit(solution)/shard_map/ppermute | solution.py:14
  92.8 0.0 copy-done.6
  92.8 0.1 add_add_fusion
  92.9 0.1 add.181
  92.9 0.6 add.178
  93.6 0.6 pad_clamp_fusion
  94.2 0.1 bitcast_reduce_fusion
  94.3 0.1 fusion.7
  94.4 1.2 compare_and_fusion
  95.6 0.6 add_rsqrt_fusion
  96.2 38.2 %collective-permute-done = bf16[1,192,3072]{2,1,0:T(8,128)(2,1)S(1)} collective-permute-done((bf16[1,192,3072]{2,1,0:T(8,128)(2,1)}, bf16[1,192,3072]{2,1,0:T(8,128)(2,1)S(1)}, u32[]{:S(2)}, u32[]{:S(2)}) %collective-permute-start) | collective-permute-done | bytes 1179680 | tf_op jit(solution)/shard_map/ppermute | solution.py:14
  134.4 1.0 fusion
  135.5 8.4 %psum.22 = f32[1,192]{1,0:T(1,128)} all-reduce(f32[1,192]{1,0:T(1,128)} %bitcast.67), channel_id=1, replica_groups=mesh['section'=8,'dp'=32,'tensor'=2] {'tensor'}, use_global_device_ids=true, to_apply=%region_6.7 | all-reduce | flops 192 | bytes 1536 | tf_op jit(solution)/shard_map/psum | solution.py:55
  143.8 0.7 add_rsqrt_fusion.2
  144.5 0.0 copy-done.4
  144.5 1.5 fusion.2
  146.0 74.2 %all-reduce.3.cloned.1.call-done = (bf16[512,3072]{1,0:T(8,128)(2,1)}, bf16[192,3072]{1,0:T(8,128)(2,1)}) async-done(((bf16[512,3072]{1,0:T(8,128)(2,1)}, bf16[192,3072]{1,0:T(8,128)(2,1)}), (bf16[512,3072]{1,0:T(8,128)(2,1)}, bf16[192,3072]{1,0:T(8,128)(2,1)})) %all-reduce.3.cloned.1.call-update) | async-done | bytes 4325392 | tf_op jit(solution)/shard_map/psum | solution.py:47
  220.2 1.1 bitcast_reduce_fusion.1
  221.3 1.1 fusion.9
  222.4 1.2 fusion.5
  223.7 0.0 copy-start.1
  223.7 1.2 gather_fusion
  224.8 1.7 convert_subtract_fusion
  (15 shorter events, 0.1 us)
Async XLA Ops:
  7.2 75.9 %copy-start = (bf16[512,768]{1,0:T(8,128)(2,1)S(1)}, bf16[512,768]{1,0:T(8,128)(2,1)}, u32[]{:S(2)}) copy-start(bf16[512,768]{1,0:T(8,128)(2,1)} %param.7) | copy-start | bytes 2359300
  7.2 75.9 %all-gather.2.cloned.1.call-start = ((), (), s32[]{:S(2)}) async-start(), calls=%async_computation | async-start | bytes 4866048 | tf_op jit(solution)/shard_map/all_gather | solution.py:41
  7.9 212.3 %all-reduce.3.cloned.1.call-start = ((), (), s32[]{:S(2)}) async-start(), calls=%async_computation.1 | async-start | bytes 8650752 | tf_op jit(solution)/shard_map/psum | solution.py:47
  89.4 3.4 %copy-start.6 = (s32[1,12]{1,0:T(1,128)S(1)}, s32[1,12]{1,0:T(1,128)}, u32[]{:S(2)}) copy-start(s32[1,12]{1,0:T(1,128)} %param.13) | copy-start | bytes 148
  89.4 4.8 %copy-start.3 = (bf16[512,384]{1,0:T(8,128)(2,1)S(1)}, bf16[512,384]{1,0:T(8,128)(2,1)}, u32[]{:S(2)}) copy-start(bf16[512,384]{1,0:T(8,128)(2,1)} %param.9) | copy-start | bytes 1179652
  89.4 45.0 %copy-start.2 = (bf16[192,3072]{1,0:T(8,128)(2,1)S(1)}, bf16[192,3072]{1,0:T(8,128)(2,1)}, u32[]{:S(2)}) copy-start(bf16[192,3072]{1,0:T(8,128)(2,1)} %param.11) | copy-start | bytes 3538948
  89.4 45.0 %collective-permute-start = (bf16[1,192,3072]{2,1,0:T(8,128)(2,1)}, bf16[1,192,3072]{2,1,0:T(8,128)(2,1)S(1)}, u32[]{:S(2)}, u32[]{:S(2)}) collective-permute-start(bf16[1,192,3072]{2,1,0:T(8,128)(2,1)} %param.10), channel_id=1, source_target_pairs={{0,64},{64,128},{128,192},{192,256},{256,320},{320,384},{384,448},... | collective-permute-start | bytes 3538952 | tf_op jit(solution)/shard_map/ppermute | solution.py:14
  93.6 50.9 %copy-start.4 = (f32[1,3072]{1,0:T(1,128)S(1)}, f32[1,3072]{1,0:T(1,128)}, u32[]{:S(2)}) copy-start(f32[1,3072]{1,0:T(1,128)} %param.12) | copy-start | bytes 36868
  146.0 78.8 %copy-start.5 = (pred[192]{0:T(512)(128)(4,1)S(1)}, pred[192]{0:T(512)(128)(4,1)}, u32[]{:S(2)}) copy-start(pred[192]{0:T(512)(128)(4,1)} %compare_and_fusion) | copy-start | bytes 580
  223.7 2.9 %copy-start.1 = (bf16[512,384]{1,0:T(8,128)(2,1)}, bf16[512,384]{1,0:T(8,128)(2,1)S(1)}, u32[]{:S(2)}) copy-start(bf16[512,384]{1,0:T(8,128)(2,1)S(1)} %fusion.5) | copy-start | bytes 1179652
Sparse Core Ops, SparseCore 0:
  10.2 72.8 all-gather.1
  89.5 130.6 all-reduce.2
where the time goes:
time: 234 us; the launch traced here: 233 us
  waiting for transfers between devices  187 us (80%)
  between operations  14.1 us (6%)
  other arithmetic  12.4 us (5%)
  blocking collectives  8.36 us (4%)
  matrix products  6.33 us (3%)
  starting transfers between devices  3.39 us (1%)
    psum x1, waiting for transfers between devices, on_device(): summed = lax.psum(partial_sum, 'section').astype(jnp.float32)  74.2 us
    all_gather x1, waiting for transfers between devices, on_device(): lax.all_gather(out_weight, 'dp', axis=1, tiled=True)  73.9 us
    ppermute x1, waiting for transfers between devices, shifted(): lax.ppermute(value, axis, [(source, source + steps) for source in range(l...  38.2 us
    psum x1, blocking collectives, on_device(): squares = lax.psum(jnp.sum(current * current, axis=-1), 'tensor')  8.36 us
    dot_general x1, matrix products, on_device(): jnp.dot(context, lax.all_gather(out_weight, 'dp', axis=1, tiled=True), pr...  6.33 us
  transfers between devices with their start and end apart: 3, of which 3 were waited for; matrix products, arithmetic and copies ran while one was open for 3% of the time, Pallas kernels for 0%

commit v1 on v0

--- a/solution.py
+++ b/solution.py
@@ -44,7 +44,7 @@
     width = previous.shape[1]
     position = lax.axis_index("section")
     sections = lax.axis_size("section")
-    summed = lax.psum(partial_sum, "section").astype(jnp.float32)
+    summed = jnp.sum(lax.all_gather(partial_sum, "section"), axis=0).astype(jnp.float32)
     share = lax.dynamic_slice_in_dim(summed, position * width, width, 1)
     images = context.shape[0] // PATCHES
     normed_new = instance_norm(share, images)

time: 234 us -> 448 us (1.91)
  waiting for transfers between devices: 187 us -> 381 us
  other arithmetic: 12.4 us -> 28.8 us
    all_gather x0 -> x1, waiting for transfers between devices: none -> 209 us  [on_device(): lax.all_gather(partial_sum, 'section')]
    reduce_sum x0 -> x1, other arithmetic: none -> 15.8 us  [on_device(): jnp.sum(lax.all_gather(partial_sum, 'section'), axis=0).astype(jnp.float32)]
    psum x1, waiting for transfers between devices: 74.2 us -> 61.5 us  [spread_2(): return lax.psum(jnp.where(mine, x, jnp.zeros_like(x)), axis)]
  transfers between devices with their start and end apart: 3 -> 4, of which waited for: 3 -> 4; matrix products, arithmetic and copies ran while one was open for 3% -> 7% of each run, Pallas kernels for 0% -> 0%
where the time goes in v1:
time: 448 us; the launch traced here: 445 us
  waiting for transfers between devices  381 us (85%)
  other arithmetic  28.8 us (6%)
  between operations  13.9 us (3%)
  blocking collectives  8.36 us (2%)
  matrix products  6.34 us (1%)
    all_gather x1, waiting for transfers between devices, on_device(): lax.all_gather(partial_sum, 'section')  209 us
    all_gather x1, waiting for transfers between devices, on_device(): lax.all_gather(out_weight, 'dp', axis=1, tiled=True)  75.1 us
    psum x1, waiting for transfers between devices, spread_2(): return lax.psum(jnp.where(mine, x, jnp.zeros_like(x)), axis)  61.5 us
    ppermute x1, waiting for transfers between devices, shifted(): lax.ppermute(value, axis, [(source, source + steps) for source in range(l...  35.3 us
    reduce_sum x1, other arithmetic, on_device(): jnp.sum(lax.all_gather(partial_sum, 'section'), axis=0).astype(jnp.float32)  15.8 us
  transfers between devices with their start and end apart: 4, of which 4 were waited for; matrix products, arithmetic and copies ran while one was open for 7% of the time, Pallas kernels for 0%

profile of v1, /device:TPU:1, one launch (start us, length us, event | category | flops | bytes accessed | tf_op | source)
XLA Modules:
  0.0 444.6 jit_solution(10136485787272507310)
XLA Ops:
  7.2 0.0 all-gather.4.cloned.1.call-start
  7.2 0.7 all-gather.4.cloned.1.call-update
  7.9 0.0 all-gather.6.cloned.1.call-start
  8.0 75.1 %all-gather.4.cloned.1.call-done = bf16[768,3072]{0,1:T(8,128)(2,1)} async-done(((bf16[768,96]{0,1:T(8,128)(2,1)}), bf16[768,3072]{0,1:T(8,128)(2,1)}) %all-gather.4.cloned.1.call-update) | async-done | bytes 4718608 | tf_op jit(solution)/shard_map/all_gather | solution.py:41
  83.1 6.3 %convolution_convert_fusion = bf16[512,3072]{1,0:T(8,128)(2,1)} fusion(bf16[512,768]{1,0:T(8,128)(2,1)S(1)} %copy-done, bf16[768,3072]{0,1:T(8,128)(2,1)} %all-gather.4.cloned.1.call-done), kind=kOutput, calls=%fused_computation.1 | convolution fusion | flops 2417491968 | bytes 8650752 | tf_op jit(solution)/shard_map/dot_general | solution.py:39
  89.4 0.0 all-gather.6.cloned.1.call-update
  89.5 0.0 all-reduce.2.cloned.1.call-start
  89.5 3.3 collective-permute-start
  92.8 1.2 select_bitcast_fusion
  94.0 0.0 all-reduce.2.cloned.1.call-update
  94.1 0.1 add_add_fusion
  94.2 0.6 add.179
  94.8 0.6 add.176
  95.4 0.7 compare_select_fusion
  96.1 0.6 pad_clamp_fusion
  96.7 0.1 bitcast_reduce_fusion
  96.8 0.1 fusion.7
  97.0 1.2 compare_and_fusion
  98.1 0.6 add_rsqrt_fusion
  98.7 35.3 %collective-permute-done = bf16[1,192,3072]{2,1,0:T(8,128)(2,1)S(1)} collective-permute-done((bf16[1,192,3072]{2,1,0:T(8,128)(2,1)}, bf16[1,192,3072]{2,1,0:T(8,128)(2,1)S(1)}, u32[]{:S(2)}, u32[]{:S(2)}) %collective-permute-start) | collective-permute-done | bytes 1179680 | tf_op jit(solution)/shard_map/ppermute | solution.py:14
  134.0 1.0 fusion
  135.1 8.4 %psum.14 = f32[1,192]{1,0:T(1,128)} all-reduce(f32[1,192]{1,0:T(1,128)} %bitcast.69), channel_id=1, replica_groups=mesh['section'=8,'dp'=32,'tensor'=2] {'tensor'}, use_global_device_ids=true, to_apply=%region_6.7 | all-reduce | flops 192 | bytes 1536 | tf_op jit(solution)/shard_map/psum | solution.py:55
  143.4 0.7 add_rsqrt_fusion.2
  144.1 1.5 fusion.2
  145.6 208.7 %all-gather.6.cloned.1.call-done = bf16[4096,3072]{1,0:T(8,128)(2,1)} async-done(((bf16[512,3072]{1,0:T(8,128)(2,1)}), bf16[4096,3072]{1,0:T(8,128)(2,1)}) %all-gather.6.cloned.1.call-update) | async-done | bytes 25165840 | tf_op jit(solution)/shard_map/all_gather | solution.py:47
  354.3 15.8 %reduce_sum.59 = bf16[512,3072]{1,0:T(8,128)(2,1)} reduce(bf16[8,512,3072]{2,1,0:T(8,128)(2,1)} %bitcast.66, bf16[]{:T(256)} %constant.77.clone.1), dimensions={0}, to_apply=%region_0.0 | reduce | flops 11010048 | bytes 28311554 | tf_op jit(solution)/shard_map/reduce_sum | solution.py:47
  370.2 1.1 bitcast_reduce_fusion.1
  371.2 1.1 fusion.9
  372.4 1.2 fusion.5
  373.6 1.2 gather_fusion
  374.8 61.5 %all-reduce.2.cloned.1.call-done = bf16[192,3072]{1,0:T(8,128)(2,1)} async-done(((bf16[192,3072]{1,0:T(8,128)(2,1)}), bf16[192,3072]{1,0:T(8,128)(2,1)}) %all-reduce.2.cloned.1.call-update) | async-done | bytes 1179664 | tf_op jit(solution)/shard_map/psum | solution.py:19
  436.3 1.7 convert_subtract_fusion
  (21 shorter events, 0.1 us)
Async XLA Ops:
  7.2 75.9 %copy-start = (bf16[512,768]{1,0:T(8,128)(2,1)S(1)}, bf16[512,768]{1,0:T(8,128)(2,1)}, u32[]{:S(2)}) copy-start(bf16[512,768]{1,0:T(8,128)(2,1)} %param.7) | copy-start | bytes 2359300
  7.2 75.9 %all-gather.4.cloned.1.call-start = ((), (), s32[]{:S(2)}) async-start(), calls=%async_computation | async-start | bytes 4866048 | tf_op jit(solution)/shard_map/all_gather | solution.py:41
  7.9 346.4 %all-gather.6.cloned.1.call-start = ((), (), s32[]{:S(2)}) async-start(), calls=%async_computation.2 | async-start | bytes 28311552 | tf_op jit(solution)/shard_map/all_gather | solution.py:47
  89.4 4.6 %copy-start.7 = (s32[1,12]{1,0:T(1,128)S(1)}, s32[1,12]{1,0:T(1,128)}, u32[]{:S(2)}) copy-start(s32[1,12]{1,0:T(1,128)} %param.13) | copy-start | bytes 148
  89.4 7.3 %copy-start.3 = (bf16[512,384]{1,0:T(8,128)(2,1)S(1)}, bf16[512,384]{1,0:T(8,128)(2,1)}, u32[]{:S(2)}) copy-start(bf16[512,384]{1,0:T(8,128)(2,1)} %param.9) | copy-start | bytes 1179652
  89.4 44.6 %copy-start.2 = (bf16[192,3072]{1,0:T(8,128)(2,1)S(1)}, bf16[192,3072]{1,0:T(8,128)(2,1)}, u32[]{:S(2)}) copy-start(bf16[192,3072]{1,0:T(8,128)(2,1)} %param.11) | copy-start | bytes 3538948
  89.5 346.9 %all-reduce.2.cloned.1.call-start = ((), (), s32[]{:S(2)}) async-start(), calls=%async_computation.1 | async-start | bytes 2359296 | tf_op jit(solution)/shard_map/psum | solution.py:19
  89.5 44.5 %collective-permute-start = (bf16[1,192,3072]{2,1,0:T(8,128)(2,1)}, bf16[1,192,3072]{2,1,0:T(8,128)(2,1)S(1)}, u32[]{:S(2)}, u32[]{:S(2)}) collective-permute-start(bf16[1,192,3072]{2,1,0:T(8,128)(2,1)} %param.10), channel_id=1, source_target_pairs={{0,64},{64,128},{128,192},{192,256},{256,320},{320,384},{384,448},... | collective-permute-start | bytes 3538952 | tf_op jit(solution)/shard_map/ppermute | solution.py:14
  95.4 48.7 %copy-start.4 = (f32[1,3072]{1,0:T(1,128)S(1)}, f32[1,3072]{1,0:T(1,128)}, u32[]{:S(2)}) copy-start(f32[1,3072]{1,0:T(1,128)} %param.12) | copy-start | bytes 36868
  354.3 18.1 %copy-start.5 = (f32[2,384]{1,0:T(2,128)S(1)}, f32[2,384]{1,0:T(2,128)}, u32[]{:S(2)}) copy-start(f32[2,384]{1,0:T(2,128)} %add_rsqrt_fusion) | copy-start | bytes 9220
  370.2 66.2 %copy-start.6 = (pred[192]{0:T(512)(128)(4,1)S(1)}, pred[192]{0:T(512)(128)(4,1)}, u32[]{:S(2)}) copy-start(pred[192]{0:T(512)(128)(4,1)} %compare_and_fusion) | copy-start | bytes 580
  373.6 64.4 %copy-start.1 = (bf16[512,384]{1,0:T(8,128)(2,1)}, bf16[512,384]{1,0:T(8,128)(2,1)S(1)}, u32[]{:S(2)}) copy-start(bf16[512,384]{1,0:T(8,128)(2,1)S(1)} %fusion.5) | copy-start | bytes 1179652
Sparse Core Ops, SparseCore 0:
  10.2 72.8 all-gather.3
  89.5 264.7 all-gather.5
  356.7 79.6 all-reduce.1
